TPU v7x, 32 devices: a whole 2x2x4 slice. The times are simulated.
32 devices in a mesh: replica: 8 (over y, x, core), fsdp: 4 (over z).
Axes of the slice: x: 2, y: 2, z: 4, core: 2. Of those that a mesh axis runs over, the one named last changes fastest.
Arguments:
- activations: bfloat16 [8, 512, 8192], P('replica', 'fsdp'), may hold values from -6 to 6
- key_grad: bfloat16 [8, 512, 512], P('replica', 'fsdp'), may hold values from -6 to 6
- inner_weight: bfloat16 [8, 512, 8192], P('replica', None, 'fsdp'), may hold values from -4 to 4
- weight_first: bfloat16 [8, 512, 8192], P('replica', None, 'fsdp'), may hold values from -0.14941406 to 0.14941406
- weight_second: bfloat16 [8, 512, 8192], P('replica', None, 'fsdp'), may hold values from 0.00062179565 to 0.012451172
- norm_gain: float32 [8, 8192], P('replica', 'fsdp'), may hold values from 0.1 to 1.9
- gain_first: float32 [8, 8192], P('replica', 'fsdp'), may hold values from -10 to 10
- gain_second: float32 [8, 8192], P('replica', 'fsdp'), may hold values from 10 to 200
- step_count: int32 [], replicated, may hold values from 1 to 19
- outer_params: float32 [512, 8192], P('replica', 'fsdp'), may hold values from -4 to 4
- outer_momentum: float32 [512, 8192], P('replica', 'fsdp'), may hold values from -3 to 3
Outputs:
- merged_weight: bfloat16 [8, 512, 8192], P('replica', None, 'fsdp')
- outer_params_new: float32 [512, 8192], P('replica', 'fsdp')
- outer_momentum_new: float32 [512, 8192], P('replica', 'fsdp')
- gain_new: float32 [8, 8192], P('replica', 'fsdp')
- gain_first_new: float32 [8, 8192], P('replica', 'fsdp')
- gain_second_new: float32 [8, 8192], P('replica', 'fsdp')
All inputs are finite; a program needn't handle non-finite values.
Results may differ from a plain program's by a relative error of at most 0.008.
Values may be sent and summed in bfloat16 or wider, within the bound.
A program may use at most 128 MiB of HBM per device.

v0:
```python
import jax
import jax.numpy as jnp
from jax import lax
from jax.sharding import PartitionSpec as P

D = 8192


BETA_ONE = 0.9
BETA_TWO = 0.95
ADAM_EPS = 1e-08
INNER_RATE = 0.25
WEIGHT_DECAY = 0.1
OUTER_RATE = 0.7
OUTER_MOMENTUM = 0.9
MIX_LOCAL = 0.5
NORM_EPS = 1e-05


def adamw(param, gradient, first_moment, second_moment, correct_first, correct_second, decay):
    first_new = BETA_ONE * first_moment + (1.0 - BETA_ONE) * gradient
    second_new = BETA_TWO * second_moment + (1.0 - BETA_TWO) * gradient * gradient
    update = (
        first_new / correct_first / (jnp.sqrt(second_new / correct_second) + ADAM_EPS)
        + decay * param
    )
    return (param - INNER_RATE * update, first_new, second_new)


def nesterov(params, momentum, average):
    change = params - average
    momentum_new = OUTER_MOMENTUM * momentum + change
    return (params - OUTER_RATE * (change + OUTER_MOMENTUM * momentum_new), momentum_new)


def shards(
    activations,
    key_grad,
    inner_weight,
    weight_first,
    weight_second,
    norm_gain,
    gain_first,
    gain_second,
    step_count,
    outer_params,
    outer_momentum,
):
    step_value = step_count.astype(jnp.float32)
    correct_first = 1.0 - jnp.power(jnp.float32(BETA_ONE), step_value)
    correct_second = 1.0 - jnp.power(jnp.float32(BETA_TWO), step_value)
    factor = D ** (-0.5)
    token_rows = activations[0].astype(jnp.float32)
    normed = (
        token_rows * lax.rsqrt(jnp.mean(token_rows * token_rows, axis=1, keepdims=True) + NORM_EPS)
    ).astype(jnp.bfloat16)
    columns = lax.all_to_all(normed, "fsdp", split_axis=1, concat_axis=0, tiled=True)
    gain_cols = norm_gain[0]
    shaped = (columns.astype(jnp.float32) * gain_cols).astype(jnp.bfloat16)
    weight = inner_weight[0]
    portion = lax.all_gather(key_grad[0], "fsdp", axis=0, tiled=True)
    weight_grad = lax.dot_general(
        portion, shaped, (((0,), (0,)), ((), ())), preferred_element_type=jnp.float32
    )
    input_grad = jnp.dot(portion, weight, preferred_element_type=jnp.float32)
    gain_grad = jnp.sum(input_grad * columns.astype(jnp.float32), axis=0)
    weight_grad, gain_grad = (weight_grad, gain_grad)
    local_weight, unused_first, unused_second = adamw(
        weight.astype(jnp.float32),
        weight_grad * factor,
        weight_first[0].astype(jnp.float32),
        weight_second[0].astype(jnp.float32),
        correct_first,
        correct_second,
        WEIGHT_DECAY,
    )
    gain_out, gain_first_out, gain_second_out = adamw(
        gain_cols,
        gain_grad * factor,
        gain_first[0],
        gain_second[0],
        correct_first,
        correct_second,
        0.0,
    )
    snapshot = weight.astype(jnp.float32)
    replicas = lax.axis_size("replica")
    total = lax.psum(snapshot.astype(jnp.bfloat16), "replica").astype(jnp.float32)
    params_full, momentum_full = (
        lax.all_gather(outer_params, "replica", axis=0, tiled=True),
        lax.all_gather(outer_momentum, "replica", axis=0, tiled=True),
    )
    params_new, momentum_new = nesterov(params_full, momentum_full, total / replicas)
    length = outer_params.shape[0]
    offset = lax.axis_index("replica") * length
    params_out = lax.dynamic_slice_in_dim(params_new, offset, length, 0)
    momentum_out = lax.dynamic_slice_in_dim(momentum_new, offset, length, 0)
    merged = (MIX_LOCAL * local_weight + (1.0 - MIX_LOCAL) * params_new).astype(jnp.bfloat16)
    return (
        merged[None],
        params_out,
        momentum_out,
        gain_out[None],
        gain_first_out[None],
        gain_second_out[None],
    )


def solution(mesh):
    return jax.shard_map(
        shards,
        mesh=mesh,
        in_specs=(
            P("replica", "fsdp", None),
            P("replica", "fsdp", None),
            P("replica", None, "fsdp"),
            P("replica", None, "fsdp"),
            P("replica", None, "fsdp"),
            P("replica", "fsdp"),
            P("replica", "fsdp"),
            P("replica", "fsdp"),
            P(),
            P("replica", "fsdp"),
            P("replica", "fsdp"),
        ),
        out_specs=(
            P("replica", None, "fsdp"),
            P("replica", "fsdp"),
            P("replica", "fsdp"),
            P("replica", "fsdp"),
            P("replica", "fsdp"),
            P("replica", "fsdp"),
        ),
        check_vma=False,
    )
```

profile of v0, /device:TPU:0, one launch (start us, length us, event | category | flops | bytes accessed | tf_op | source)
XLA Modules:
  0.0 186.6 jit_solution(7084771831853737114)
XLA Ops:
  7.2 0.0 copy-start
  7.2 0.0 all-gather.6.cloned.1.call-start
  7.2 0.7 all-gather.6.cloned.1.call-update
  7.9 0.0 all-gather.4.cloned.1.call-start
  8.0 0.7 all-gather.4.cloned.1.call-update
  8.7 6.0 %reshape.69 = f32[128,4,2048]{2,1,0:T(4,128)} reshape(bf16[1,128,8192]{2,1,0:T(8,128)(2,1)} %param.11) | data formatting | bytes 6291456 | tf_op jit(solution)/shard_map/convert_element_type | solution.py:53
  14.7 0.0 copy-done
  14.7 0.5 multiply_reduce_fusion
  15.2 5.8 %fusion.12 = bf16[128,4,2048]{2,0,1:T(8,128)(2,1)} fusion(f32[128,4,2048]{2,1,0:T(4,128)} %reshape.69, f32[128]{0:T(128)S(1)} %add_rsqrt_fusion), kind=kLoop, calls=%fused_computation.19 | loop fusion | flops 2097152 | bytes 6291968 | tf_op jit(solution)/shard_map/convert_element_type | solution.py:56
  20.9 6.3 %all-to-all-start = ((bf16[128,4,2048]{2,0,1:T(8,128)(2,1)}), bf16[128,4,2048]{2,0,1:T(8,128)(2,1)S(1)}, u32[]{:S(2)}, u32[]{:S(2)}) async-start(bf16[128,4,2048]{2,0,1:T(8,128)(2,1)} %fusion.12), calls=%async_computation | async-start | bytes 4194304 | tf_op jit(solution)/shard_map/all_to_all | solution.py:57
  27.3 0.0 all-reduce.2.cloned.1.call-start
  27.3 3.9 %copy.26 = bf16[1,512,2048]{1,2,0:T(8,128)(2,1)} copy(bf16[1,512,2048]{2,1,0:T(8,128)(2,1)} %param.13) | data formatting | bytes 4194304 | tf_op args[2]
  31.2 0.0 all-reduce.2.cloned.1.call-update
  31.9 0.0 copy-start.4
  31.9 4.0 %copy.27 = bf16[1,512,2048]{1,2,0:T(8,128)(2,1)} copy(bf16[1,512,2048]{2,1,0:T(8,128)(2,1)} %param.14) | data formatting | bytes 4194304 | tf_op args[3]
  36.0 3.9 %copy.29 = bf16[1,512,2048]{1,2,0:T(8,128)(2,1)} copy(bf16[1,512,2048]{2,1,0:T(8,128)(2,1)} %param.15) | data formatting | bytes 4194304 | tf_op args[4]
  39.9 0.0 copy-done.4
  39.9 45.8 %all-gather = bf16[1,512,512]{2,1,0:T(8,128)(2,1)S(1)} all-gather(bf16[1,128,512]{2,1,0:T(8,128)(2,1)S(1)} %copy-done.4), channel_id=2, replica_groups=mesh['replica'=8,'fsdp'=4] {'fsdp'}, dimensions={1}, use_global_device_ids=true | all-gather | bytes 655360 | tf_op jit(solution)/shard_map/all_gather | solution.py:61
  85.7 0.0 copy-start.3
  85.7 0.0 copy-start.5
  85.7 0.0 copy-start.6
  85.7 0.0 copy-start.7
  85.7 0.0 all-to-all-done
  85.7 3.1 %fusion.6 = f32[2048]{0:T(1024)S(1)} fusion(bf16[128,4,2048]{2,0,1:T(8,128)(2,1)S(1)} %all-to-all-done, bf16[1,512,2048]{2,1,0:T(8,128)(2,1)} %param.13, bf16[1,512,512]{2,1,0:T(8,128)(2,1)S(1)} %all-gather), kind=kOutput, calls=%fused_computation.10 | convolution fusion | flops 1076885504 | bytes 4726784 | tf_op jit(solution)/shard_map/dot_general | solution.py:65
  88.8 0.0 copy-done.3
  88.8 0.0 copy-done.5
  88.8 0.0 copy-done.6
  88.8 0.0 copy-done.7
  88.8 0.7 multiply_subtract_fusion.2
  89.5 1.7 fusion.5
  91.2 0.0 all-gather.6.cloned.1.call-done
  91.2 5.4 %copy.31 = f32[512,2048]{0,1:T(8,128)} copy(f32[512,2048]{1,0:T(8,128)} %all-gather.6.cloned.1.call-done) | data formatting | bytes 8388608 | tf_op jit(solution)/shard_map/all_gather | solution.py:91
  96.6 0.0 all-gather.4.cloned.1.call-done
  96.6 5.5 %copy.32 = f32[512,2048]{0,1:T(8,128)} copy(f32[512,2048]{1,0:T(8,128)} %all-gather.4.cloned.1.call-done) | data formatting | bytes 8388608 | tf_op jit(solution)/shard_map/all_gather | solution.py:90
  102.1 51.1 %all-reduce.2.cloned.1.call-done = bf16[512,2048]{0,1:T(8,128)(2,1)} async-done(((bf16[512,2048]{0,1:T(8,128)(2,1)}), bf16[512,2048]{0,1:T(8,128)(2,1)}) %all-reduce.2.cloned.1.call-update) | async-done | bytes 2097168 | tf_op jit(solution)/shard_map/psum | solution.py:88
  153.3 5.3 %multiply_add_fusion = (f32[512,2048]{0,1:T(8,128)S(1)}, f32[512,2048]{0,1:T(8,128)S(1)}) fusion(f32[512,2048]{0,1:T(8,128)} %copy.31, f32[512,2048]{0,1:T(8,128)} %copy.32, bf16[512,2048]{0,1:T(8,128)(2,1)} %all-reduce.2.cloned.1.call-done), kind=kLoop, calls=%fused_computation.21 | loop fusion | flops 9437184 | bytes 18874368 | tf_op jit(solution)/shard_map/add | solution.py:32
  158.6 0.0 copy-start.2
  158.6 0.0 copy-start.1
  158.7 2.1 %copy-done.2 = f32[512,2048]{0,1:T(8,128)} copy-done((f32[512,2048]{0,1:T(8,128)}, f32[512,2048]{0,1:T(8,128)S(1)}, u32[]{:S(2)}) %copy-start.2) | copy-done | bytes 4194328
  160.8 1.6 constant_dynamic-slice_fusion
  162.3 2.3 %copy.34 = f32[64,2048]{1,0:T(8,128)} copy(f32[64,2048]{0,1:T(8,128)} %get-tuple-element.26) | data formatting | bytes 1048576
  164.7 1.1 copy.35
  165.8 0.0 copy-done.1
  165.8 10.4 %fusion.14 = bf16[1,512,2048]{1,2,0:T(8,128)(2,1)} fusion(f32[512,2048]{0,1:T(8,128)} %copy-done.2, f32[]{:T(128)S(6)} %sub.20, bf16[1,512,2048]{1,2,0:T(8,128)(2,1)} %copy.29, f32[]{:T(128)S(6)} %sub.19, bf16[1,512,2048]{1,2,0:T(8,128)(2,1)} %copy.27, bf16[512,2048]{1,0:T(8,128)(2,1)} %fusion.5, bf16[1,512,512]{2,1,0:T(8,128)(2,1)} %copy-done.3, ...), kind=kOutput, calls=%fused_computation.25 | convolution fusion | flops 1096810496 | bytes 15204360 | tf_op jit(solution)/shard_map/dot_general | solution.py:62
  176.2 3.9 %copy.33 = bf16[1,512,2048]{2,1,0:T(8,128)(2,1)} copy(bf16[1,512,2048]{1,2,0:T(8,128)(2,1)} %fusion.14) | data formatting | bytes 4194304
  (2 shorter events, 0.0 us)
Async XLA Ops:
  7.2 7.5 %copy-start = (bf16[1,128,8192]{2,1,0:T(8,128)(2,1)S(1)}, bf16[1,128,8192]{2,1,0:T(8,128)(2,1)}, u32[]{:S(2)}) copy-start(bf16[1,128,8192]{2,1,0:T(8,128)(2,1)} %param.11) | copy-start | bytes 6291460
  7.2 84.0 %all-gather.6.cloned.1.call-start = ((), (), s32[]{:S(2)}) async-start(), calls=%async_computation.3 | async-start | bytes 4718592 | tf_op jit(solution)/shard_map/all_gather | solution.py:91
  7.9 88.7 %all-gather.4.cloned.1.call-start = ((), (), s32[]{:S(2)}) async-start(), calls=%async_computation.1 | async-start | bytes 4718592 | tf_op jit(solution)/shard_map/all_gather | solution.py:90
  20.9 64.7 %all-to-all-start = ((bf16[128,4,2048]{2,0,1:T(8,128)(2,1)}), bf16[128,4,2048]{2,0,1:T(8,128)(2,1)S(1)}, u32[]{:S(2)}, u32[]{:S(2)}) async-start(bf16[128,4,2048]{2,0,1:T(8,128)(2,1)} %fusion.12), calls=%async_computation | async-start | bytes 4194304 | tf_op jit(solution)/shard_map/all_to_all | solution.py:57
  27.3 126.0 %all-reduce.2.cloned.1.call-start = ((), (), s32[]{:S(2)}) async-start(), calls=%async_computation.2 | async-start | bytes 4194304 | tf_op jit(solution)/shard_map/psum | solution.py:88
  31.9 7.9 %copy-start.4 = (bf16[1,128,512]{2,1,0:T(8,128)(2,1)S(1)}, bf16[1,128,512]{2,1,0:T(8,128)(2,1)}, u32[]{:S(2)}) copy-start(bf16[1,128,512]{2,1,0:T(8,128)(2,1)} %param.12) | copy-start | bytes 393220
  85.7 3.1 %copy-start.3 = (bf16[1,512,512]{2,1,0:T(8,128)(2,1)}, bf16[1,512,512]{2,1,0:T(8,128)(2,1)S(1)}, u32[]{:S(2)}) copy-start(bf16[1,512,512]{2,1,0:T(8,128)(2,1)S(1)} %all-gather) | copy-start | bytes 1572868
  85.7 3.1 %copy-start.5 = (f32[1,2048]{1,0:T(1,128)S(1)}, f32[1,2048]{1,0:T(1,128)}, u32[]{:S(2)}) copy-start(f32[1,2048]{1,0:T(1,128)} %param.16) | copy-start | bytes 24580
  85.7 3.1 %copy-start.6 = (f32[1,2048]{1,0:T(1,128)S(1)}, f32[1,2048]{1,0:T(1,128)}, u32[]{:S(2)}) copy-start(f32[1,2048]{1,0:T(1,128)} %param.18) | copy-start | bytes 24580
  85.7 3.1 %copy-start.7 = (f32[1,2048]{1,0:T(1,128)S(1)}, f32[1,2048]{1,0:T(1,128)}, u32[]{:S(2)}) copy-start(f32[1,2048]{1,0:T(1,128)} %param.17) | copy-start | bytes 24580
  158.6 2.1 %copy-start.2 = (f32[512,2048]{0,1:T(8,128)}, f32[512,2048]{0,1:T(8,128)S(1)}, u32[]{:S(2)}) copy-start(f32[512,2048]{0,1:T(8,128)S(1)} %get-tuple-element.22) | copy-start | bytes 12582916
  158.6 7.1 %copy-start.1 = (bf16[1,512,2048]{1,2,0:T(8,128)(2,1)S(1)}, bf16[1,512,2048]{1,2,0:T(8,128)(2,1)}, u32[]{:S(2)}) copy-start(bf16[1,512,2048]{1,2,0:T(8,128)(2,1)} %copy.26) | copy-start | bytes 6291460
Sparse Core Ops, SparseCore 0:
  9.9 39.4 all-gather.5
  51.2 36.7 all-gather.3
  91.8 61.4 all-reduce.1
where the time goes:
time: 187 us
  waiting for transfers between devices  52.5 us (28%)
  blocking collectives  45.8 us (24%)
  local copies, waits for them, and re-layouts  39.8 us (21%)
  between operations  14.6 us (8%)
  other arithmetic  14 us (7%)
  matrix products  13.5 us (7%)
  starting transfers between devices  6.4 us (3%)
    psum x1, waiting for transfers between devices, shards(): lax.psum(snapshot.astype(jnp.bfloat16), 'replica').astype(jnp.float32)  51.1 us
    all_gather x1, blocking collectives, shards(): portion = lax.all_gather(key_grad[0], 'fsdp', axis=0, tiled=True)  45.8 us
    unnamed x22, local copies, waits for them, and re-layouts  21.3 us
    dot_general x1, matrix products, shards(): lax.dot_general(portion, shaped, (((0,), (0,)), ((), ())), preferred_elem...  10.4 us
    all_to_all x1, starting transfers between devices, shards(): lax.all_to_all(normed, 'fsdp', split_axis=1, concat_axis=0, tiled=True)  6.32 us
    convert_element_type x1, local copies, waits for them, and re-layouts, shards(): token_rows = activations[0].astype(jnp.float32)  6.01 us
    convert_element_type x1, other arithmetic, shards(): normed = (token_rows * lax.rsqrt(jnp.mean(token_rows * token_rows, axis=1...  5.76 us
    all_gather x1, local copies, waits for them, and re-layouts, shards(): lax.all_gather(outer_params, 'replica', axis=0, tiled=True)  5.54 us
  transfers between devices with their start and end apart: 4, of which 1 were waited for; matrix products, arithmetic and copies ran while one was open for 22% of the time, Pallas kernels for 0%

commit v1 on v0

v1 whole, which is shorter than its diff:
```python
import functools
import math

import jax
import jax.numpy as jnp
from jax import lax
from jax.experimental import pallas as pl
from jax.experimental.pallas import tpu as pltpu
from jax.sharding import PartitionSpec as P

BETA_ONE = 0.9
BETA_TWO = 0.95
ADAM_EPS = 1e-08
INNER_RATE = 0.25
WEIGHT_DECAY = 0.1
OUTER_RATE = 0.7
OUTER_MOMENTUM = 0.9
MIX_LOCAL = 0.5
NORM_EPS = 1e-05

MESH = pl.DeviceIdType.MESH
F32 = jnp.float32
BF16 = jnp.bfloat16


def kernel(
    n_f,
    n_r,
    chunk,
    step_ref,
    act,
    key,
    weight,
    first,
    second,
    gain,
    gfirst,
    gsecond,
    outer,
    momentum,
    merged_out,
    outer_out,
    momentum_out,
    gain_out,
    gfirst_out,
    gsecond_out,
    x_own,
    x_all,
    k_own,
    k_scaled,
    k_all,
    w_buf,
    m_buf,
    v_buf,
    g_buf,
    merged,
    pair_in,
    pair_sum,
    rs_in,
    par_all,
    outer_buf,
    mom_buf,
    outer_new,
    mom_new,
    gains,
    gains_new,
    local_sem,
    out_sem,
    act_send,
    act_recv,
    k_send,
    k_recv,
    pair_send,
    pair_recv,
    rs_send,
    rs_recv,
    ag_send,
    ag_recv,
    fw_send,
    fw_recv,
):
    tokens = act.shape[1]
    width = act.shape[2]
    cols = weight.shape[2]
    features = weight.shape[1]
    rows = outer.shape[0]
    chunks = cols // chunk
    chips = n_r // 2
    factor = width ** (-0.5)

    me_f = lax.axis_index("fsdp")
    me_r = lax.axis_index("replica")
    chip, core = me_r // 2, me_r % 2
    mate = chip * 2 + 1 - core

    def peer_f(offset):
        return lax.rem(me_f + offset + n_f, n_f)

    def peer_chip(offset):
        return lax.rem(chip + offset + chips, chips)

    def to_f(index):
        return (me_r, index)

    def to_r(index):
        return (index, me_f)

    def row_block(index):
        return pl.ds(pl.multiple_of(index * rows, rows), rows)

    def tok_block(index):
        return pl.ds(pl.multiple_of(index * tokens, tokens), tokens)

    def chunk_cols(j):
        return pl.ds(pl.multiple_of(j * chunk, chunk), chunk)

    loads = [
        pltpu.make_async_copy(act.at[0], x_own, local_sem.at[0]),
        pltpu.make_async_copy(key.at[0], k_own, local_sem.at[1]),
        pltpu.make_async_copy(weight.at[0], w_buf, local_sem.at[2]),
        pltpu.make_async_copy(outer, outer_buf, local_sem.at[3]),
        pltpu.make_async_copy(momentum, mom_buf, local_sem.at[4]),
        pltpu.make_async_copy(
            act.at[0, :, pl.ds(pl.multiple_of(me_f * cols, cols), cols)],
            x_all.at[tok_block(me_f), :],
            local_sem.at[5],
        ),
        pltpu.make_async_copy(first.at[0], m_buf, local_sem.at[6]),
        pltpu.make_async_copy(second.at[0], v_buf, local_sem.at[7]),
        pltpu.make_async_copy(gain, gains.at[0], local_sem.at[8]),
        pltpu.make_async_copy(gfirst, gains.at[1], local_sem.at[9]),
        pltpu.make_async_copy(gsecond, gains.at[2], local_sem.at[10]),
    ]
    for load in loads:
        load.start()

    barrier = pltpu.get_barrier_semaphore()
    for offset in range(1, n_f):
        pl.semaphore_signal(barrier, inc=1, device_id=to_f(peer_f(offset)), device_id_type=MESH)
    for offset in range(1, chips):
        pl.semaphore_signal(
            barrier, inc=1, device_id=to_r(peer_chip(offset) * 2 + core), device_id_type=MESH
        )
    pl.semaphore_signal(barrier, inc=1, device_id=to_r(mate), device_id_type=MESH)
    pl.semaphore_wait(barrier, n_f + chips - 1)

    def act_copy(offset, j):
        target = peer_f(offset)
        start = pl.multiple_of(target * cols + j * chunk, chunk)
        return pltpu.make_async_remote_copy(
            src_ref=act.at[0, :, pl.ds(start, chunk)],
            dst_ref=x_all.at[tok_block(me_f), chunk_cols(j)],
            send_sem=act_send.at[offset - 1, j],
            recv_sem=act_recv.at[offset - 1, j],
            device_id=to_f(target),
            device_id_type=MESH,
        )

    def act_arrival(offset, j):
        source = peer_f(-offset)
        return pltpu.make_async_remote_copy(
            src_ref=act.at[0, :, chunk_cols(j)],
            dst_ref=x_all.at[tok_block(source), chunk_cols(j)],
            send_sem=act_send.at[offset - 1, j],
            recv_sem=act_recv.at[offset - 1, j],
            device_id=to_f(source),
            device_id_type=MESH,
        )

    offsets = sorted(range(1, n_f), key=lambda o: (abs(o - n_f / 2), o))

    def send_chunk(j):
        for offset in offsets:
            act_copy(offset, j).start()

    send_chunk(0)

    def pair_copy(c):
        return pltpu.make_async_remote_copy(
            src_ref=weight.at[0, row_block(2 * c + 1 - core), :],
            dst_ref=pair_in.at[c],
            send_sem=pair_send.at[c],
            recv_sem=pair_recv.at[c],
            device_id=to_r(mate),
            device_id_type=MESH,
        )

    for c in range(chips):
        pair_copy(c).start()

    loads[0].wait()
    loads[1].wait()

    def norm_rows(i, carry):
        at = pl.ds(pl.multiple_of(i * 16, 16), 16)
        total = jnp.zeros((16, 1), F32)
        for piece in range(width // 1024):
            x = x_own[at, piece * 1024 : (piece + 1) * 1024].astype(F32)
            total += jnp.sum(x * x, axis=1, keepdims=True)
        scale = lax.rsqrt(total / width + NORM_EPS)
        k_scaled[at, :] = k_own[at, :].astype(F32) * scale
        return carry

    lax.fori_loop(0, tokens // 16, norm_rows, 0)
    k_all[:, tok_block(me_f)] = k_scaled[...].T.astype(BF16)

    def key_copy(offset, owner, target):
        return pltpu.make_async_remote_copy(
            src_ref=k_all.at[:, tok_block(owner)],
            dst_ref=k_all.at[:, tok_block(owner)],
            send_sem=k_send.at[offset - 1],
            recv_sem=k_recv.at[offset - 1],
            device_id=to_f(target),
            device_id_type=MESH,
        )

    for offset in offsets:
        key_copy(offset, me_f, peer_f(offset)).start()
    lax.fori_loop(1, chunks, lambda j, carry: (send_chunk(j), carry)[1], 0)

    def rs_copy(offset):
        target = peer_chip(offset)
        return pltpu.make_async_remote_copy(
            src_ref=pair_sum.at[target],
            dst_ref=rs_in.at[chip],
            send_sem=rs_send.at[offset - 1],
            recv_sem=rs_recv.at[offset - 1],
            device_id=to_r(target * 2 + core),
            device_id_type=MESH,
        )

    def rs_arrival(offset):
        source = peer_chip(-offset)
        return pltpu.make_async_remote_copy(
            src_ref=pair_sum.at[source],
            dst_ref=rs_in.at[source],
            send_sem=rs_send.at[offset - 1],
            recv_sem=rs_recv.at[offset - 1],
            device_id=to_r(source * 2 + core),
            device_id_type=MESH,
        )

    loads[2].wait()
    for c in range(chips):
        pair_copy(c).wait_recv()

    for offset in list(range(1, chips)) + [0]:
        target = peer_chip(offset)

        def add_rows(i, carry, target=target):
            at = pl.ds(pl.multiple_of(i * 16, 16), 16)
            own = pl.ds(pl.multiple_of((2 * target + core) * rows + i * 16, 16), 16)
            pair_sum[target, at, :] = (
                w_buf[own, :].astype(F32) + pair_in[target, at, :].astype(F32)
            ).astype(BF16)
            return carry

        lax.fori_loop(0, rows // 16, add_rows, 0)
        if offset:
            rs_copy(offset).start()

    loads[3].wait()
    loads[4].wait()
    for offset in range(1, chips):
        rs_arrival(offset).wait_recv()

    def outer_rows(i, carry):
        at = pl.ds(pl.multiple_of(i * 16, 16), 16)
        own = pl.ds(pl.multiple_of(me_r * rows + i * 16, 16), 16)
        piece = min(512, cols)
        for p in range(cols // piece):
            cs = slice(p * piece, (p + 1) * piece)
            total = pair_sum[chip, at, cs].astype(F32)
            for offset in range(1, chips):
                total += rs_in[peer_chip(offset), at, cs].astype(F32)
            params = outer_buf[at, cs]
            change = params - total / n_r
            mom = OUTER_MOMENTUM * mom_buf[at, cs] + change
            new = params - OUTER_RATE * (change + OUTER_MOMENTUM * mom)
            mom_new[at, cs] = mom
            outer_new[at, cs] = new
            par_all[own, cs] = new.astype(BF16)
        return carry

    lax.fori_loop(0, rows // 16, outer_rows, 0)

    def ag_copy(offset, owner, target):
        return pltpu.make_async_remote_copy(
            src_ref=par_all.at[row_block(owner), :],
            dst_ref=par_all.at[row_block(owner), :],
            send_sem=ag_send.at[offset - 1],
            recv_sem=ag_recv.at[offset - 1],
            device_id=to_r(target),
            device_id_type=MESH,
        )

    def fw_copy(offset, owner):
        return pltpu.make_async_remote_copy(
            src_ref=par_all.at[row_block(owner), :],
            dst_ref=par_all.at[row_block(owner), :],
            send_sem=fw_send.at[offset],
            recv_sem=fw_recv.at[offset],
            device_id=to_r(mate),
            device_id_type=MESH,
        )

    for offset in range(1, chips):
        ag_copy(offset, me_r, peer_chip(offset) * 2 + core).start()
    fw_copy(0, me_r).start()
    outs = [
        pltpu.make_async_copy(outer_new, outer_out, out_sem.at[0]),
        pltpu.make_async_copy(mom_new, momentum_out, out_sem.at[1]),
    ]
    for out in outs:
        out.start()
    for offset in range(1, chips):
        owner = peer_chip(-offset) * 2 + core
        ag_copy(offset, owner, owner).wait_recv()
        fw_copy(offset, owner).start()

    for load in loads[5:]:
        load.wait()
    for offset in offsets:
        source = peer_f(-offset)
        key_copy(offset, source, source).wait_recv()
    for offset in range(chips):
        fw_copy(offset, peer_chip(-offset) * 2 + 1 - core).wait_recv()

    step_value = jnp.full((1, chunk), step_ref[0], jnp.int32).astype(F32)
    inv_first = 1.0 / (1.0 - jnp.exp(step_value * math.log(BETA_ONE)))
    inv_second = 1.0 / (1.0 - jnp.exp(step_value * math.log(BETA_TWO)))
    tile = 32

    def merged_copy(j):
        return pltpu.make_async_copy(
            merged.at[:, chunk_cols(j)], merged_out.at[0, :, chunk_cols(j)], out_sem.at[5 + j]
        )

    def do_chunk(j, carry):
        for offset in offsets:
            act_arrival(offset, j).wait_recv()
        cs = chunk_cols(j)
        g_buf[...] = jnp.dot(k_all[...], x_all[:, cs], preferred_element_type=F32)
        gain_cols = gains[0, :, cs]
        scale = gain_cols * factor

        def do_rows(i, total):
            at = pl.ds(pl.multiple_of(i * tile, tile), tile)
            g = g_buf[at, :]
            w = w_buf[at, cs].astype(F32)
            prod = g * w
            for s in range(tile // 8):
                total += prod[s * 8 : (s + 1) * 8, :]
            grad = g * scale
            m = BETA_ONE * m_buf[at, cs].astype(F32) + (1.0 - BETA_ONE) * grad
            v = BETA_TWO * v_buf[at, cs].astype(F32) + (1.0 - BETA_TWO) * grad * grad
            update = (m * inv_first) / (jnp.sqrt(v * inv_second) + ADAM_EPS) + WEIGHT_DECAY * w
            local = w - INNER_RATE * update
            new = MIX_LOCAL * local + (1.0 - MIX_LOCAL) * par_all[at, cs].astype(F32)
            merged[at, cs] = new.astype(BF16)
            return total

        total = lax.fori_loop(0, features // tile, do_rows, jnp.zeros((8, chunk), F32))
        merged_copy(j).start()
        grad = jnp.sum(total, axis=0, keepdims=True) * factor
        m = BETA_ONE * gains[1, :, cs] + (1.0 - BETA_ONE) * grad
        v = BETA_TWO * gains[2, :, cs] + (1.0 - BETA_TWO) * grad * grad
        gains_new[0, :, cs] = gain_cols - INNER_RATE * (
            (m * inv_first) / (jnp.sqrt(v * inv_second) + ADAM_EPS)
        )
        gains_new[1, :, cs] = m
        gains_new[2, :, cs] = v
        return carry

    lax.fori_loop(0, chunks, do_chunk, 0)

    gain_outs = [
        pltpu.make_async_copy(gains_new.at[0], gain_out, out_sem.at[2]),
        pltpu.make_async_copy(gains_new.at[1], gfirst_out, out_sem.at[3]),
        pltpu.make_async_copy(gains_new.at[2], gsecond_out, out_sem.at[4]),
    ]
    for out in gain_outs:
        out.start()

    for offset in offsets:
        key_copy(offset, me_f, peer_f(offset)).wait_send()

    def drain(j, carry):
        for offset in offsets:
            act_copy(offset, j).wait_send()
        merged_copy(j).wait()
        return carry

    for c in range(chips):
        pair_copy(c).wait_send()
        fw_copy(c, me_r).wait_send()
    for offset in range(1, chips):
        rs_copy(offset).wait_send()
        ag_copy(offset, me_r, peer_chip(offset) * 2 + core).wait_send()
    lax.fori_loop(0, chunks, drain, 0)
    for out in outs + gain_outs:
        out.wait()


def shards(
    n_f,
    n_r,
    activations,
    key_grad,
    inner_weight,
    weight_first,
    weight_second,
    norm_gain,
    gain_first,
    gain_second,
    step_count,
    outer_params,
    outer_momentum,
):
    tokens, width = activations.shape[1:]
    features, cols = inner_weight.shape[1:]
    rows = outer_params.shape[0]
    chips = n_r // 2
    chunk = min(256, cols)
    chunks = cols // chunk
    dma = pltpu.SemaphoreType.DMA
    any_spec = pl.BlockSpec(memory_space=pl.ANY)
    return pl.pallas_call(
        functools.partial(kernel, n_f, n_r, chunk),
        out_shape=(
            jax.ShapeDtypeStruct(inner_weight.shape, BF16),
            jax.ShapeDtypeStruct(outer_params.shape, F32),
            jax.ShapeDtypeStruct(outer_params.shape, F32),
            jax.ShapeDtypeStruct(norm_gain.shape, F32),
            jax.ShapeDtypeStruct(norm_gain.shape, F32),
            jax.ShapeDtypeStruct(norm_gain.shape, F32),
        ),
        in_specs=[pl.BlockSpec(memory_space=pltpu.SMEM)] + [any_spec] * 10,
        out_specs=(any_spec,) * 6,
        scratch_shapes=[
            pltpu.VMEM((tokens, width), BF16),
            pltpu.VMEM((n_f * tokens, cols), BF16),
            pltpu.VMEM((tokens, features), BF16),
            pltpu.VMEM((tokens, features), F32),
            pltpu.VMEM((features, n_f * tokens), BF16),
            pltpu.VMEM((features, cols), BF16),
            pltpu.VMEM((features, cols), BF16),
            pltpu.VMEM((features, cols), BF16),
            pltpu.VMEM((features, chunk), F32),
            pltpu.VMEM((features, cols), BF16),
            pltpu.VMEM((chips, rows, cols), BF16),
            pltpu.VMEM((chips, rows, cols), BF16),
            pltpu.VMEM((chips, rows, cols), BF16),
            pltpu.VMEM((features, cols), BF16),
            pltpu.VMEM((rows, cols), F32),
            pltpu.VMEM((rows, cols), F32),
            pltpu.VMEM((rows, cols), F32),
            pltpu.VMEM((rows, cols), F32),
            pltpu.VMEM((3, 1, cols), F32),
            pltpu.VMEM((3, 1, cols), F32),
            dma((11,)),
            dma((5 + chunks,)),
            dma((n_f - 1, chunks)),
            dma((n_f - 1, chunks)),
            dma((n_f - 1,)),
            dma((n_f - 1,)),
            dma((chips,)),
            dma((chips,)),
            dma((chips - 1,)),
            dma((chips - 1,)),
            dma((chips - 1,)),
            dma((chips - 1,)),
            dma((chips,)),
            dma((chips,)),
        ],
        compiler_params=pltpu.CompilerParams(
            collective_id=0, has_side_effects=True, vmem_limit_bytes=48 * 1024 * 1024
        ),
        name="diloco_step",
    )(
        step_count.reshape(1),
        activations,
        key_grad,
        inner_weight,
        weight_first,
        weight_second,
        norm_gain,
        gain_first,
        gain_second,
        outer_params,
        outer_momentum,
    )


def solution(mesh):
    return jax.shard_map(
        functools.partial(shards, mesh.shape["fsdp"], mesh.shape["replica"]),
        mesh=mesh,
        in_specs=(
            P("replica", "fsdp", None),
            P("replica", "fsdp", None),
            P("replica", None, "fsdp"),
            P("replica", None, "fsdp"),
            P("replica", None, "fsdp"),
            P("replica", "fsdp"),
            P("replica", "fsdp"),
            P("replica", "fsdp"),
            P(),
            P("replica", "fsdp"),
            P("replica", "fsdp"),
        ),
        out_specs=(
            P("replica", None, "fsdp"),
            P("replica", "fsdp"),
            P("replica", "fsdp"),
            P("replica", "fsdp"),
            P("replica", "fsdp"),
            P("replica", "fsdp"),
        ),
        check_vma=False,
    )
```

time: 187 us -> 76.5 us (0.41)
  Pallas kernels: 0 us -> 65.1 us
  waiting for transfers between devices: 52.5 us -> 0 us
  blocking collectives: 45.8 us -> 0 us
  local copies, waits for them, and re-layouts: 39.8 us -> 9.77 us
  other arithmetic: 14 us -> 0 us
  matrix products: 13.5 us -> 0 us
  between operations: 14.6 us -> 1.31 us
  starting transfers between devices: 6.4 us -> 0 us
    pallas_call x0 -> x1, Pallas kernels: none -> 65.1 us  [shards(): pl.pallas_call(functools.partial(kernel, n_f, n_r, chunk), out_shape=(jax...]
    psum x1 -> x0, waiting for transfers between devices: 51.1 us -> none  [shards(): lax.psum(snapshot.astype(jnp.bfloat16), 'replica').astype(jnp.float32)]
    all_gather x1 -> x0, blocking collectives: 45.8 us -> none  [shards(): portion = lax.all_gather(key_grad[0], 'fsdp', axis=0, tiled=True)]
    dot_general x2 -> x0, matrix products: 13.5 us -> none  [the longest x1 10.4 us: shards(): lax.dot_general(portion, shaped, (((0,), (0,)), ((), ())), preferred_elem...]
    unnamed x22 -> x18, local copies, waits for them, and re-layouts: 21.3 us -> 9.77 us
    all_gather x2 -> x0, local copies, waits for them, and re-layouts: 10.9 us -> none  [the longest x1 5.54 us: shards(): lax.all_gather(outer_params, 'replica', axis=0, tiled=True)]
    convert_element_type x2 -> x0, other arithmetic: 7.51 us -> none  [the longest x1 5.76 us: shards(): normed = (token_rows * lax.rsqrt(jnp.mean(token_rows * token_rows, axis=1...]
    all_to_all x1 -> x0, starting transfers between devices: 6.32 us -> none  [shards(): lax.all_to_all(normed, 'fsdp', split_axis=1, concat_axis=0, tiled=True)]
  transfers between devices with their start and end apart: 4 -> 0, of which waited for: 1 -> 0; matrix products, arithmetic and copies ran while one was open for 22% -> 0% of each run, Pallas kernels for 0% -> 0%
where the time goes in v1:
time: 76.5 us; the launch traced here: 76.2 us
  Pallas kernels  65.1 us (85%)
  local copies, waits for them, and re-layouts  9.77 us (13%)
  between operations  1.31 us (2%)
    pallas_call x1, Pallas kernels, shards(): pl.pallas_call(functools.partial(kernel, n_f, n_r, chunk), out_shape=(jax...  65.1 us
    unnamed x18, local copies, waits for them, and re-layouts  9.77 us

profile of v1, /device:TPU:0, one launch (start us, length us, event | category | flops | bytes accessed | tf_op | source)
XLA Modules:
  0.0 76.2 jit_solution(5636375922179111247)
XLA Ops:
  1.3 0.0 copy-start
  1.3 1.0 %copy-done = f32[64,2048]{1,0:T(8,128)S(1)} copy-done((f32[64,2048]{1,0:T(8,128)S(1)}, f32[64,2048]{1,0:T(8,128)}, u32[]{:S(2)}) %copy-start) | copy-done | bytes 524312
  2.3 0.0 copy-start.1
  2.3 1.0 %copy-done.1 = f32[64,2048]{1,0:T(8,128)S(1)} copy-done((f32[64,2048]{1,0:T(8,128)S(1)}, f32[64,2048]{1,0:T(8,128)}, u32[]{:S(2)}) %copy-start.1) | copy-done | bytes 524312
  3.4 0.0 copy-start.2
  3.4 0.9 %copy-done.2 = bf16[1,128,512]{2,1,0:T(8,128)(2,1)S(1)} copy-done((bf16[1,128,512]{2,1,0:T(8,128)(2,1)S(1)}, bf16[1,128,512]{2,1,0:T(8,128)(2,1)}, u32[]{:S(2)}) %copy-start.2) | copy-done | bytes 131096
  4.3 0.0 copy-start.3
  4.3 0.7 copy-done.3
  5.0 0.0 copy-start.4
  5.0 0.7 copy-done.4
  5.7 0.0 copy-start.5
  5.7 0.7 copy-done.5
  6.4 65.1 %diloco_step.1 = (bf16[1,512,2048]{2,1,0:T(8,128)(2,1)S(1)}, f32[64,2048]{1,0:T(8,128)S(1)}, f32[64,2048]{1,0:T(8,128)S(1)}, f32[1,2048]{1,0:T(1,128)S(1)}, f32[...) custom-call(s32[1]{0:T(128)} %bitcast.1.step_ref, bf16[1,128,8192]{2,1,0:T(8,128)(2,1)} %act.1, ...), custom_call_target="tpu_custom_call" | custom-call | tf_op jit(solution)/shard_map/diloco_step/pallas_call | solution.py:428
  71.5 1.3 %copy.24 = bf16[1,512,2048]{2,1,0:T(8,128)(2,1)} copy(bf16[1,512,2048]{2,1,0:T(8,128)(2,1)S(1)} %get-tuple-element.12) | data formatting | bytes 4194304
  72.8 0.8 %copy.25 = f32[64,2048]{1,0:T(8,128)} copy(f32[64,2048]{1,0:T(8,128)S(1)} %get-tuple-element.13) | data formatting | bytes 1048576
  73.6 0.8 %copy.26 = f32[64,2048]{1,0:T(8,128)} copy(f32[64,2048]{1,0:T(8,128)S(1)} %get-tuple-element.14) | data formatting | bytes 1048576
  74.4 0.6 copy.27
  75.0 0.6 copy.28
  75.6 0.6 copy.29
Async XLA Ops:
  1.3 1.0 %copy-start = (f32[64,2048]{1,0:T(8,128)S(1)}, f32[64,2048]{1,0:T(8,128)}, u32[]{:S(2)}) copy-start(f32[64,2048]{1,0:T(8,128)} %outer.1) | copy-start | bytes 1572868
  2.3 1.0 %copy-start.1 = (f32[64,2048]{1,0:T(8,128)S(1)}, f32[64,2048]{1,0:T(8,128)}, u32[]{:S(2)}) copy-start(f32[64,2048]{1,0:T(8,128)} %momentum.1) | copy-start | bytes 1572868
  3.4 0.9 %copy-start.2 = (bf16[1,128,512]{2,1,0:T(8,128)(2,1)S(1)}, bf16[1,128,512]{2,1,0:T(8,128)(2,1)}, u32[]{:S(2)}) copy-start(bf16[1,128,512]{2,1,0:T(8,128)(2,1)} %key.1) | copy-start | bytes 393220
  4.3 0.7 copy-start.3
  5.0 0.7 copy-start.4
  5.7 0.7 copy-start.5

commit v2 on v1

--- a/solution.py
+++ b/solution.py
@@ -21,6 +21,7 @@
 MESH = pl.DeviceIdType.MESH
 F32 = jnp.float32
 BF16 = jnp.bfloat16
+VMEM_LIMIT = 60 * 1024 * 1024
 
 
 def kernel(
@@ -87,6 +88,7 @@
     chunks = cols // chunk
     chips = n_r // 2
     factor = width ** (-0.5)
+    early = min(2, chunks)
 
     me_f = lax.axis_index("fsdp")
     me_r = lax.axis_index("replica")
@@ -131,8 +133,6 @@
         pltpu.make_async_copy(gfirst, gains.at[1], local_sem.at[9]),
         pltpu.make_async_copy(gsecond, gains.at[2], local_sem.at[10]),
     ]
-    for load in loads:
-        load.start()
 
     barrier = pltpu.get_barrier_semaphore()
     for offset in range(1, n_f):
@@ -142,6 +142,8 @@
             barrier, inc=1, device_id=to_r(peer_chip(offset) * 2 + core), device_id_type=MESH
         )
     pl.semaphore_signal(barrier, inc=1, device_id=to_r(mate), device_id_type=MESH)
+    for load in loads:
+        load.start()
     pl.semaphore_wait(barrier, n_f + chips - 1)
 
     def act_copy(offset, j):
@@ -204,19 +206,42 @@
     lax.fori_loop(0, tokens // 16, norm_rows, 0)
     k_all[:, tok_block(me_f)] = k_scaled[...].T.astype(BF16)
 
-    def key_copy(offset, owner, target):
+    def key_copy(owner, step):
         return pltpu.make_async_remote_copy(
             src_ref=k_all.at[:, tok_block(owner)],
             dst_ref=k_all.at[:, tok_block(owner)],
-            send_sem=k_send.at[offset - 1],
-            recv_sem=k_recv.at[offset - 1],
-            device_id=to_f(target),
-            device_id_type=MESH,
-        )
-
-    for offset in offsets:
-        key_copy(offset, me_f, peer_f(offset)).start()
-    lax.fori_loop(1, chunks, lambda j, carry: (send_chunk(j), carry)[1], 0)
+            send_sem=k_send.at[(step + 1) // 2, owner],
+            recv_sem=k_recv.at[owner],
+            device_id=to_f(peer_f(step)),
+            device_id_type=MESH,
+        )
+
+    @pl.when(me_f < n_f - 1)
+    def _():
+        key_copy(me_f, 1).start()
+
+    @pl.when(me_f > 0)
+    def _():
+        key_copy(me_f, -1).start()
+
+    lax.fori_loop(1, early, lambda j, carry: (send_chunk(j), carry)[1], 0)
+
+    def pass_keys(distance):
+        @pl.when(me_f >= distance)
+        def _():
+            key_copy(me_f - distance, 1).wait_recv()
+
+            @pl.when(me_f < n_f - 1)
+            def _():
+                key_copy(me_f - distance, 1).start()
+
+        @pl.when(me_f + distance < n_f)
+        def _():
+            key_copy(me_f + distance, -1).wait_recv()
+
+            @pl.when(me_f > 0)
+            def _():
+                key_copy(me_f + distance, -1).start()
 
     def rs_copy(offset):
         target = peer_chip(offset)
@@ -258,6 +283,10 @@
         lax.fori_loop(0, rows // 16, add_rows, 0)
         if offset:
             rs_copy(offset).start()
+
+    for distance in range(1, n_f - 1):
+        pass_keys(distance)
+    lax.fori_loop(early, chunks, lambda j, carry: (send_chunk(j), carry)[1], 0)
 
     loads[3].wait()
     loads[4].wait()
@@ -320,9 +349,7 @@
 
     for load in loads[5:]:
         load.wait()
-    for offset in offsets:
-        source = peer_f(-offset)
-        key_copy(offset, source, source).wait_recv()
+    pass_keys(n_f - 1)
     for offset in range(chips):
         fw_copy(offset, peer_chip(-offset) * 2 + 1 - core).wait_recv()
 
@@ -382,8 +409,16 @@
     for out in gain_outs:
         out.start()
 
-    for offset in offsets:
-        key_copy(offset, me_f, peer_f(offset)).wait_send()
+    for owner in range(n_f):
+
+        @pl.when(jnp.logical_and(me_f >= owner, me_f < n_f - 1))
+        def _(owner=owner):
+            key_copy(owner, 1).wait_send()
+
+        @pl.when(jnp.logical_and(me_f <= owner, me_f > 0))
+        def _(owner=owner):
+            key_copy(owner, -1).wait_send()
+
 
     def drain(j, carry):
         for offset in offsets:
@@ -400,6 +435,17 @@
     lax.fori_loop(0, chunks, drain, 0)
     for out in outs + gain_outs:
         out.wait()
+
+
+def hand_over(*refs):
+    sem = refs[-1]
+    copies = [
+        pltpu.make_async_copy(refs[i], refs[6 + i], sem.at[i]) for i in range(6)
+    ]
+    for copy in copies:
+        copy.start()
+    for copy in copies:
+        copy.wait()
 
 
 def shards(
@@ -425,7 +471,7 @@
     chunks = cols // chunk
     dma = pltpu.SemaphoreType.DMA
     any_spec = pl.BlockSpec(memory_space=pl.ANY)
-    return pl.pallas_call(
+    results = pl.pallas_call(
         functools.partial(kernel, n_f, n_r, chunk),
         out_shape=(
             jax.ShapeDtypeStruct(inner_weight.shape, BF16),
@@ -462,8 +508,8 @@
             dma((5 + chunks,)),
             dma((n_f - 1, chunks)),
             dma((n_f - 1, chunks)),
-            dma((n_f - 1,)),
-            dma((n_f - 1,)),
+            dma((2, n_f)),
+            dma((n_f,)),
             dma((chips,)),
             dma((chips,)),
             dma((chips - 1,)),
@@ -474,7 +520,7 @@
             dma((chips,)),
         ],
         compiler_params=pltpu.CompilerParams(
-            collective_id=0, has_side_effects=True, vmem_limit_bytes=48 * 1024 * 1024
+            collective_id=0, has_side_effects=True, vmem_limit_bytes=VMEM_LIMIT
         ),
         name="diloco_step",
     )(
@@ -490,6 +536,14 @@
         outer_params,
         outer_momentum,
     )
+    return pl.pallas_call(
+        hand_over,
+        out_shape=tuple(jax.ShapeDtypeStruct(r.shape, r.dtype) for r in results),
+        in_specs=[pl.BlockSpec(memory_space=pltpu.VMEM)] * 6,
+        out_specs=(any_spec,) * 6,
+        scratch_shapes=[dma((6,))],
+        name="hand_over",
+    )(*results)
 
 
 def solution(mesh):

time: 76.5 us -> 64.7 us (0.85)
  local copies, waits for them, and re-layouts: 9.77 us -> 0 us
  Pallas kernels: 65.1 us -> 63.3 us
    unnamed x18 -> x0, local copies, waits for them, and re-layouts: 9.77 us -> none
    pallas_call x1, Pallas kernels: 65.1 us -> 59.7 us  [shards(): pl.pallas_call(functools.partial(kernel, n_f, n_r, chunk), out_shape=(jax...]
    pallas_call x0 -> x1, Pallas kernels: none -> 3.57 us  [shards(): pl.pallas_call(hand_over, out_shape=tuple((jax.ShapeDtypeStruct(r.shape,...]
where the time goes in v2:
time: 64.7 us; the launch traced here: 64.6 us
  Pallas kernels  63.3 us (98%)
  between operations  1.29 us (2%)
    pallas_call x1, Pallas kernels, shards(): pl.pallas_call(functools.partial(kernel, n_f, n_r, chunk), out_shape=(jax...  59.7 us
    pallas_call x1, Pallas kernels, shards(): pl.pallas_call(hand_over, out_shape=tuple((jax.ShapeDtypeStruct(r.shape,...  3.57 us

profile of v2, /device:TPU:0, one launch (start us, length us, event | category | flops | bytes accessed | tf_op | source)
XLA Modules:
  0.0 64.6 jit_solution(3514789459979776295)
XLA Ops:
  1.3 59.7 %diloco_step.1 = (bf16[1,512,2048]{2,1,0:T(8,128)(2,1)}, f32[64,2048]{1,0:T(8,128)}, f32[64,2048]{1,0:T(8,128)}, f32[1,2048]{1,0:T(1,128)}, f32[1,2048]{1,0:T(1,128)}, /*index=5*/f32[1,2048]{1,0:T(1,128)}) custom-call(s32[1]{0:T(128)} %bitcast.1.step_ref, bf16[1,128,8192]{2,1,0:T(8,128)(2,1)} %act.1, bf16[1,128,512]{2,1,0:T(8,128)(2,1)} %key.1, ...), custom_call_target="tpu_custom_call" | custom-call | tf_op jit(solution)/shard_map/diloco_step/pallas_call | solution.py:474
  61.0 3.6 %hand_over.1 = (bf16[1,512,2048]{2,1,0:T(8,128)(2,1)}, f32[64,2048]{1,0:T(8,128)}, f32[64,2048]{1,0:T(8,128)}, f32[1,2048]{1,0:T(1,128)}, f32[1,2048]{1,0:T(1,128)}, /*index=5*/f32[1,2048]{1,0:T(1,128)}) custom-call(bf16[1,512,2048]{2,1,0:T(8,128)(2,1)} %get-tuple-element.12.refs_0_, f32[64,2048]{1,0:T(8,128)} %get-tuple-element.13.refs_1_, ...), custom_call_target="tpu_custom_call" | custom-call | tf_op jit(solution)/shard_map/hand_over/pallas_call | solution.py:539

commit v3 on v2

--- a/solution.py
+++ b/solution.py
@@ -89,6 +89,7 @@
     chips = n_r // 2
     factor = width ** (-0.5)
     early = min(2, chunks)
+    later = min(3, chunks)
 
     me_f = lax.axis_index("fsdp")
     me_r = lax.axis_index("replica")
@@ -284,9 +285,11 @@
         if offset:
             rs_copy(offset).start()
 
-    for distance in range(1, n_f - 1):
+    pass_keys(1)
+    lax.fori_loop(early, later, lambda j, carry: (send_chunk(j), carry)[1], 0)
+    for distance in range(2, n_f - 1):
         pass_keys(distance)
-    lax.fori_loop(early, chunks, lambda j, carry: (send_chunk(j), carry)[1], 0)
+    lax.fori_loop(later, chunks, lambda j, carry: (send_chunk(j), carry)[1], 0)
 
     loads[3].wait()
     loads[4].wait()
@@ -438,14 +441,23 @@
 
 
 def hand_over(*refs):
-    sem = refs[-1]
-    copies = [
-        pltpu.make_async_copy(refs[i], refs[6 + i], sem.at[i]) for i in range(6)
-    ]
-    for copy in copies:
-        copy.start()
-    for copy in copies:
-        copy.wait()
+    sources, targets, buffers, (in_sem, out_sem) = refs[:6], refs[6:12], refs[12:18], refs[18:]
+    features = sources[0].shape[1]
+    pieces = [(0, (0, pl.ds(i * (features // 4), features // 4))) for i in range(4)]
+    pieces += [(i, (slice(None),)) for i in range(1, 6)]
+    moves = []
+    for n, (i, at) in enumerate(pieces):
+        moves.append((
+            pltpu.make_async_copy(sources[i].at[at], buffers[i].at[at], in_sem.at[n]),
+            pltpu.make_async_copy(buffers[i].at[at], targets[i].at[at], out_sem.at[n]),
+        ))
+    for load, _ in moves:
+        load.start()
+    for load, store in moves:
+        load.wait()
+        store.start()
+    for _, store in moves:
+        store.wait()
 
 
 def shards(
@@ -539,9 +551,10 @@
     return pl.pallas_call(
         hand_over,
         out_shape=tuple(jax.ShapeDtypeStruct(r.shape, r.dtype) for r in results),
-        in_specs=[pl.BlockSpec(memory_space=pltpu.VMEM)] * 6,
+        in_specs=[any_spec] * 6,
         out_specs=(any_spec,) * 6,
-        scratch_shapes=[dma((6,))],
+        scratch_shapes=[pltpu.VMEM(r.shape, r.dtype) for r in results] + [dma((9,)), dma((9,))],
+        compiler_params=pltpu.CompilerParams(vmem_limit_bytes=VMEM_LIMIT),
         name="hand_over",
     )(*results)
 

time: 64.7 us -> 64.2 us (level)
    pallas_call x1, Pallas kernels: 3.57 us -> 2.86 us  [shards(): pl.pallas_call(hand_over, out_shape=tuple((jax.ShapeDtypeStruct(r.shape,...]
where the time goes in v3:
time: 64.2 us; the launch traced here: 64.1 us
  Pallas kernels  62.8 us (98%)
  between operations  1.29 us (2%)
    pallas_call x1, Pallas kernels, shards(): pl.pallas_call(functools.partial(kernel, n_f, n_r, chunk), out_shape=(jax...  59.9 us
    pallas_call x1, Pallas kernels, shards(): pl.pallas_call(hand_over, out_shape=tuple((jax.ShapeDtypeStruct(r.shape,...  2.86 us

profile of v3, /device:TPU:0, one launch (start us, length us, event | category | flops | bytes accessed | tf_op | source)
XLA Modules:
  0.0 64.1 jit_solution(12073099937195717444)
XLA Ops:
  1.3 59.9 %diloco_step.1 = (bf16[1,512,2048]{2,1,0:T(8,128)(2,1)}, f32[64,2048]{1,0:T(8,128)}, f32[64,2048]{1,0:T(8,128)}, f32[1,2048]{1,0:T(1,128)}, f32[1,2048]{1,0:T(1,128)}, /*index=5*/f32[1,2048]{1,0:T(1,128)}) custom-call(s32[1]{0:T(128)} %bitcast.1.step_ref, bf16[1,128,8192]{2,1,0:T(8,128)(2,1)} %act.1, bf16[1,128,512]{2,1,0:T(8,128)(2,1)} %key.1, ...), custom_call_target="tpu_custom_call" | custom-call | tf_op jit(solution)/shard_map/diloco_step/pallas_call | solution.py:486
  61.2 2.9 %hand_over.1 = (bf16[1,512,2048]{2,1,0:T(8,128)(2,1)}, f32[64,2048]{1,0:T(8,128)}, f32[64,2048]{1,0:T(8,128)}, f32[1,2048]{1,0:T(1,128)}, f32[1,2048]{1,0:T(1,128)}, /*index=5*/f32[1,2048]{1,0:T(1,128)}) custom-call(bf16[1,512,2048]{2,1,0:T(8,128)(2,1)} %get-tuple-element.12.refs_0_, f32[64,2048]{1,0:T(8,128)} %get-tuple-element.13.refs_1_, ...), custom_call_target="tpu_custom_call" | custom-call | tf_op jit(solution)/shard_map/hand_over/pallas_call | solution.py:551
